TPU v7x, 32 devices: a whole 2x2x4 slice. The times are simulated.
32 devices in a mesh: bricks: 8 (over z, x), groups: 4 (over y, core).
Axes of the slice: x: 2, y: 2, z: 4, core: 2. Of those that a mesh axis runs over, the one named last changes fastest.
Arguments:
- fields: bfloat16 [4, 48, 64, 512], P('groups', 'bricks'), may hold values from -6 to 6
- cotangent: bfloat16 [4, 48, 64, 512], P('groups', 'bricks'), may hold values from -6 to 6
- first_weight: bfloat16 [64, 1728], replicated, may hold values from -0.15625 to 0.15625
- second_weight: bfloat16 [64, 1728], replicated, may hold values from -0.15625 to 0.15625
- counts: int32 [4, 8], P('groups', 'bricks'), may hold values from 2 to 6, as said below
- adjacency: int32 [4, 48, 6], P('groups', 'bricks'), may hold values from -1 to 47, as said below
Outputs:
- grad_fields: bfloat16 [4, 48, 64, 512], P('groups', 'bricks')
- grad_first: float32 [64, 1728], replicated
- grad_second: float32 [64, 1728], replicated
Inputs may be any that keep to these rules, and one draw needn't show every extreme that they name: `counts`: each group has some slab with 6 live bricks; live bricks fill the first slots of a slab. `adjacency`: entries point only to live slots and only from live slots; the relation is symmetric (slot t is the upper neighbour of s along k exactly when s is the lower neighbour of t); the lower neighbour along the first dimension lies in the same slab or the slab one index below, the upper one in the same slab or one index above; neighbours along the second and third dimensions lie in the same slab.
All inputs are finite; a program needn't handle non-finite values.
Results may differ from a plain program's by a relative error of at most 0.0049.
Values may be sent and summed in bfloat16 or wider, within the bound.
A program may use at most 128 MiB of HBM per device.

v0:
```python
import functools

import jax
import jax.numpy as jnp
from jax import lax
from jax.experimental import pallas as pl
from jax.experimental.pallas import tpu as pltpu
from jax.sharding import PartitionSpec as P

S = 8
LANES = 128
BF = jnp.bfloat16
F32 = jnp.float32
MESH = pl.DeviceIdType.MESH


def chunk(j):
    return slice(j * LANES, (j + 1) * LANES)


def shifted(own, nbr, width, step, coord):
    if step > 0:
        return jnp.where(
            coord == 7, pltpu.roll(nbr, 7 * width, 1), pltpu.roll(own, LANES - width, 1)
        )
    return jnp.where(
        coord == 0, pltpu.roll(nbr, LANES - 7 * width, 1), pltpu.roll(own, width, 1)
    )


def level_kernel(
    count_ref, adj_ref, f_ref, c_ref, w1_ref, w2_ref, w3_ref,
    out_ref, g1_ref, g2_ref,
    base, fx, t_ref, x9, zc, zd, f3, h3, y_ref, gate, hidden, halo0, halo1, halo2, halo3,
    send_sem, recv_sem,
):
    slots, channels, cells = f_ref.shape
    count = cells // LANES
    b = lax.axis_index("bricks")
    last = lax.axis_size("bricks") - 1
    has_low, has_up = b > 0, b < last
    rows = 3 * channels
    halos = (halo0, halo1, halo2, halo3)
    barrier = pltpu.get_barrier_semaphore()

    @pl.when(has_low)
    def _():
        pl.semaphore_signal(barrier, inc=1, device_id={"bricks": b - 1}, device_id_type=MESH)

    @pl.when(has_up)
    def _():
        pl.semaphore_signal(barrier, inc=1, device_id={"bricks": b + 1}, device_id_type=MESH)

    def lanes(r):
        return lax.broadcasted_iota(jnp.int32, (r, LANES), 1)

    def local(s, k, step):
        n = adj_ref[s, 2 * k + (1 if step > 0 else 0)]
        return jnp.where(n < 0, slots, jnp.clip(n - b * slots, 0, slots))

    def across(s, step):
        n = adj_ref[s, 1 if step > 0 else 0]
        return jnp.where(n < 0, 3 * slots, jnp.clip(n - (b - 1) * slots, 0, 3 * slots))

    def copies(k):
        own = halos[k].at[pl.ds(slots, slots)]
        low = pltpu.make_async_remote_copy(
            src_ref=own, dst_ref=halos[k].at[pl.ds(2 * slots, slots)],
            send_sem=send_sem.at[k, 0], recv_sem=recv_sem.at[k, 0],
            device_id={"bricks": b - 1}, device_id_type=MESH,
        )
        up = pltpu.make_async_remote_copy(
            src_ref=own, dst_ref=halos[k].at[pl.ds(0, slots)],
            send_sem=send_sem.at[k, 1], recv_sem=recv_sem.at[k, 1],
            device_id={"bricks": b + 1}, device_id_type=MESH,
        )
        return low, up

    def send(k):
        low, up = copies(k)

        @pl.when(has_low)
        def _():
            low.start()

        @pl.when(has_up)
        def _():
            up.start()

    def arrive(k):
        low, up = copies(k)

        @pl.when(has_low)
        def _():
            low.wait_send()
            up.wait_recv()

        @pl.when(has_up)
        def _():
            up.wait_send()
            low.wait_recv()

    def each_slot(body):
        def step(s, carry):
            body(s)
            return carry

        lax.fori_loop(0, slots, step, 0)

    def stage(src, dst, s, k, parts, nrows):
        width = 8 if k == 1 else 1
        lane = lanes(nrows)
        coord = (lane // width) % 8
        low, up = local(s, k, -1), local(s, k, 1)
        for j in range(parts):
            own = src[s, :, chunk(j)]
            dst[0:nrows, chunk(j)] = shifted(own, src[low, :, chunk(j)], width, -1, coord)
            dst[nrows:2 * nrows, chunk(j)] = own
            dst[2 * nrows:3 * nrows, chunk(j)] = shifted(
                own, src[up, :, chunk(j)], width, 1, coord
            )

    def swap(a_low, a_high):
        return pltpu.roll(jnp.where(lanes(channels) < 64, a_low, a_high), 64, 1)

    def edges(first, final):
        return jnp.where(lanes(channels) < 64, first, final).astype(BF)

    def combine(s, k, j):
        zero, minus, plus = channels, 0, 2 * channels
        y_zero = y_ref[k, s, zero:zero + channels, chunk(j)]
        plus_here = y_ref[k, s, plus:plus + channels, chunk(j)]
        minus_here = y_ref[k, s, minus:minus + channels, chunk(j)]
        if j + 1 < count:
            plus_next = y_ref[k, s, plus:plus + channels, chunk(j + 1)]
        else:
            plus_next = halos[1 + 2 * k][across(s, 1)].astype(F32)
        if j > 0:
            minus_before = y_ref[k, s, minus:minus + channels, chunk(j - 1)]
        else:
            minus_before = halos[1 + 2 * k][across(s, -1)].astype(F32)
        return y_zero + swap(plus_next + minus_here, plus_here + minus_before)

    for k in range(4):
        halos[k][3 * slots] = jnp.zeros((channels, LANES), BF)

    @pl.when(jnp.logical_not(has_low))
    def _():
        for k in range(4):
            halos[k][pl.ds(0, slots)] = jnp.zeros((slots, channels, LANES), BF)

    @pl.when(jnp.logical_not(has_up))
    def _():
        for k in range(4):
            halos[k][pl.ds(2 * slots, slots)] = jnp.zeros((slots, channels, LANES), BF)

    base[slots] = jnp.zeros((channels, cells), BF)
    fx[slots] = jnp.zeros((channels, cells + LANES), BF)
    t_ref[slots] = jnp.zeros((rows, cells + LANES), BF)

    def mask_fields(s):
        keep = jnp.where(s < count_ref[0, 0], 1.0, 0.0).astype(F32)
        f = (f_ref[s].astype(F32) * keep).astype(BF)
        f3[s, channels:2 * channels, :] = f
        halos[0][slots + s] = edges(f[:, chunk(0)], f[:, chunk(count - 1)])
        base[s] = (c_ref[s].astype(F32) * keep).astype(BF)

    each_slot(mask_fields)

    pl.semaphore_wait(barrier, has_low.astype(jnp.int32) + has_up.astype(jnp.int32))
    send(0)

    def back_conv(k, w_ref, z_ref):
        each_slot(lambda s: stage(base, t_ref.at[s], s, 2, count, channels))

        def second(s):
            stage(t_ref, z_ref.at[s], s, 1, count, rows)
            y = jnp.dot(w_ref[...], z_ref[s], preferred_element_type=F32)
            y_ref[k, s] = y
            halos[1 + 2 * k][slots + s] = edges(
                y[2 * channels:, chunk(0)], y[:channels, chunk(count - 1)]
            )

        each_slot(second)
        send(1 + 2 * k)

    back_conv(0, w2_ref, zc)
    arrive(0)

    def widen(s):
        f = [f3[s, channels:2 * channels, chunk(j)] for j in range(count)]
        low, up = halos[0][across(s, -1)], halos[0][across(s, 1)]
        wide = [low] + f + [up]
        for j in range(count + 1):
            part = swap(wide[j + 1], wide[j])
            fx[s, :, chunk(j)] = part
            if j < count:
                f3[s, 0:channels, chunk(j)] = part
            if j > 0:
                f3[s, 2 * channels:3 * channels, chunk(j - 1)] = part

    each_slot(widen)
    each_slot(lambda s: stage(fx, t_ref.at[s], s, 1, count + 1, channels))

    def forward(s):
        stage(t_ref, x9, s, 2, count + 1, rows)
        y = jnp.dot(w1_ref[...], x9[...], preferred_element_type=F32)
        y_minus, y_zero, y_plus = y[:channels], y[channels:2 * channels], y[2 * channels:]
        h = []
        for j in range(count):
            pre = (
                y_minus[:, chunk(j)]
                + swap(y_zero[:, chunk(j + 1)], y_zero[:, chunk(j)])
                + y_plus[:, chunk(j + 1)]
            )
            sig = jax.nn.sigmoid(pre)
            gate[s, :, chunk(j)] = sig * (1.0 + pre * (1.0 - sig))
            h.append((pre * sig).astype(BF))
            hidden[s, :, chunk(j)] = h[-1]
        halos[2][slots + s] = edges(h[0], h[-1])

    each_slot(forward)
    send(2)
    arrive(1)

    def d_pre(s):
        for j in range(count):
            base[s, :, chunk(j)] = (combine(s, 0, j) * gate[s, :, chunk(j)]).astype(BF)

    each_slot(d_pre)
    back_conv(1, w3_ref, zd)
    arrive(2)

    def widen_hidden(s):
        h = [hidden[s, :, chunk(j)] for j in range(count)]
        wide = [halos[2][across(s, -1)]] + h + [halos[2][across(s, 1)]]
        for j in range(count + 1):
            part = swap(wide[j + 1], wide[j])
            if j < count:
                h3[s, 0:channels, chunk(j)] = part
                h3[s, channels:2 * channels, chunk(j)] = h[j]
            if j > 0:
                h3[s, 2 * channels:3 * channels, chunk(j - 1)] = part

    each_slot(widen_hidden)
    g1_ref[...] = jnp.zeros_like(g1_ref)
    g2_ref[...] = jnp.zeros_like(g2_ref)

    def weight_grads(s):
        nt = (((1,), (1,)), ((), ()))
        g2_ref[...] += lax.dot_general(zc[s], h3[s], nt, preferred_element_type=F32)
        g1_ref[...] += lax.dot_general(zd[s], f3[s], nt, preferred_element_type=F32)

    each_slot(weight_grads)
    arrive(3)

    def finish(s):
        for j in range(count):
            out_ref[s, :, chunk(j)] = combine(s, 1, j).astype(BF)

    each_slot(finish)


def on_device(fields, cotangent, first_weight, second_weight, counts, adjacency):
    slots, channels, cells = fields.shape[1:]
    w1 = first_weight.reshape(channels, channels, 3, 3, 3)
    w2 = second_weight.reshape(channels, channels, 3, 3, 3)
    rows, cols = 3 * channels, 9 * channels
    forward_w = jnp.transpose(w1, (2, 0, 4, 3, 1)).reshape(rows, cols)

    def backward_w(w):
        return jnp.transpose(jnp.flip(w, (2, 3, 4)), (2, 1, 3, 4, 0)).reshape(rows, cols)

    vmem = pl.BlockSpec(memory_space=pltpu.VMEM)
    smem = pl.BlockSpec(memory_space=pltpu.SMEM)
    grad_fields, g1, g2 = pl.pallas_call(
        level_kernel,
        out_shape=(
            jax.ShapeDtypeStruct((slots, channels, cells), BF),
            jax.ShapeDtypeStruct((cols, rows), F32),
            jax.ShapeDtypeStruct((cols, rows), F32),
        ),
        in_specs=[smem, smem] + [vmem] * 5,
        out_specs=(vmem, vmem, vmem),
        scratch_shapes=[
            pltpu.VMEM((slots + 1, channels, cells), BF),
            pltpu.VMEM((slots + 1, channels, cells + LANES), BF),
            pltpu.VMEM((slots + 1, rows, cells + LANES), BF),
            pltpu.VMEM((cols, cells + LANES), BF),
            pltpu.VMEM((slots, cols, cells), BF),
            pltpu.VMEM((slots, cols, cells), BF),
            pltpu.VMEM((slots, rows, cells), BF),
            pltpu.VMEM((slots, rows, cells), BF),
            pltpu.VMEM((2, slots, rows, cells), F32),
            pltpu.VMEM((slots, channels, cells), F32),
            pltpu.VMEM((slots, channels, cells), BF),
        ]
        + [pltpu.VMEM((3 * slots + 1, channels, LANES), BF)] * 4
        + [
            pltpu.SemaphoreType.DMA((4, 2)),
            pltpu.SemaphoreType.DMA((4, 2)),
        ],
        compiler_params=pltpu.CompilerParams(
            collective_id=0, has_side_effects=True, vmem_limit_bytes=50 * 1024 * 1024
        ),
    )(
        counts, adjacency[0], fields[0], cotangent[0],
        forward_w, backward_w(w2), backward_w(w1),
    )
    s1, s2 = lax.psum((g1, g2), ("bricks", "groups"))
    total = lax.axis_size("groups") * slots * lax.axis_size("bricks") * cells
    factor = 1.0 / jnp.sqrt(jnp.float32(total))

    def weight_out(g):
        g = jnp.flip(g.reshape(3, 3, channels, 3, channels), (0, 1)) * factor
        return jnp.transpose(g, (2, 4, 3, 0, 1)).reshape(channels, channels * 27)

    return (grad_fields[None], weight_out(s1), weight_out(s2))


def solution(mesh):
    return jax.shard_map(
        on_device,
        mesh=mesh,
        in_specs=(
            P("groups", "bricks", None, None),
            P("groups", "bricks", None, None),
            P(),
            P(),
            P("groups", "bricks"),
            P("groups", "bricks", None),
        ),
        out_specs=(P("groups", "bricks", None, None), P(), P()),
        check_vma=False,
    )
```

profile of v0, /device:TPU:1, one launch (start us, length us, event | category | flops | bytes accessed | tf_op | source)
XLA Modules:
  0.0 202.3 jit_solution(11422407175044799028)
XLA Ops:
  7.2 0.0 copy-start.3
  7.2 0.0 all-reduce.3.cloned.1.call-start
  7.9 0.7 copy.27
  8.6 1.2 copy.14
  9.9 0.3 reshape.33
  10.1 0.0 copy-done.3
  10.1 0.3 copy.16
  10.4 0.3 reshape.35
  10.7 1.7 rev.14
  12.5 0.2 copy.17
  12.7 0.4 reshape.36.w2_ref
  13.1 1.7 rev.15
  14.8 1.0 copy.15
  15.8 0.4 reshape.34.w1_ref
  16.2 0.0 copy-start
  16.3 0.0 copy-start.1
  16.3 0.2 copy.18
  16.5 0.4 reshape.37.w3_ref
  16.9 0.4 copy-done
  17.2 0.1 copy-done.1
  17.4 21.8 %shard_map.85 = (bf16[6,64,512]{2,1,0:T(8,128)(2,1)S(1)}, f32[576,192]{1,0:T(8,128)S(1)}, f32[576,192]{1,0:T(8,128)S(1)}) custom-call(s32[1,1]{1,0:T(1,128)S(6)} %copy.31.count_ref, s32[6,6]{1,0:T(8,128)S(1)} %bitcast.28, bf16[6,64,512]{2,1,0:T(8,128)(2,1)S(1)} %bitcast.26, bf16[6,64,512]{2,1,0:T(8,128)(2,1)S(1)} %bitcast.27, ...), custom_call_target="tpu_custom_call" | custom-call | tf_op jit(solution)/shard_map/pallas_call | solution.py:276
  39.2 1.0 copy.19
  40.2 0.2 copy.21
  40.4 0.5 reshape.40
  41.0 0.0 copy-start.2
  41.0 3.6 %rev.17 = f32[3,3,64,3,64]{2,1,0,4,3:T(4,128)} reverse(f32[3,3,64,3,64]{2,1,0,4,3:T(4,128)S(1)} %reshape.40), dimensions={0,1} | reverse | bytes 884736 | tf_op jit(solution)/shard_map/jit(_flip)/rev | solution.py:315
  44.5 0.0 copy-done.2
  44.5 0.5 reshape.38
  45.1 3.7 %rev.16 = f32[3,3,64,3,64]{2,1,0,4,3:T(4,128)} reverse(f32[3,3,64,3,64]{2,1,0,4,3:T(4,128)S(1)} %reshape.38), dimensions={0,1} | reverse | bytes 884736 | tf_op jit(solution)/shard_map/jit(_flip)/rev | solution.py:315
  48.8 0.0 all-reduce.3.cloned.1.call-update
  48.8 138.3 %all-reduce.3.cloned.1.call-done = (f32[3,3,64,3,64]{2,1,0,4,3:T(4,128)}, f32[3,3,64,3,64]{2,1,0,4,3:T(4,128)}) async-done(((f32[3,3,64,3,64]{2,1,0,4,3:T(4,128)}, f32[3,3,64,3,64]{2,1,0,4,3:T(4,128)}), (f32[3,3,64,3,64]{2,1,0,4,3:T(4,128)}, f32[3,3,64,3,64]{2,1,0,4,3:T(4,128)})) %all-reduce.3.cloned.1.call-update) | async-done | bytes 884752 | tf_op jit(solution)/shard_map/psum | solution.py:310
  187.1 2.2 %multiply_bitcast_fusion = (f32[64,64,3,3,3]{0,4,3,1,2:T(4,128)S(1)}, f32[64,64,3,3,3]{0,4,3,1,2:T(4,128)S(1)}) fusion(f32[3,3,64,3,64]{2,1,0,4,3:T(4,128)} %get-tuple-element.13, f32[3,3,64,3,64]{2,1,0,4,3:T(4,128)} %get-tuple-element.12), kind=kLoop, calls=%fused_computation | loop fusion | flops 221184 | bytes 1769472 | tf_op jit(solution)/shard_map/transpose | solution.py:316
  189.3 0.2 copy.22
  189.5 1.3 reshape.41
  190.9 2.2 %copy.24 = f32[64,1728]{1,0:T(8,128)} copy(f32[64,1728]{0,1:T(8,128)} %reshape.41) | data formatting | bytes 884736
  193.1 0.2 copy.20
  193.3 0.4 reshape.39
  193.7 1.1 copy.23
  194.8 0.7 copy.32
Async XLA Ops:
  7.2 3.0 %copy-start.3 = (bf16[64,1728]{1,0:T(8,128)(2,1)S(1)}, bf16[64,1728]{1,0:T(8,128)(2,1)}, u32[]{:S(2)}) copy-start(bf16[64,1728]{1,0:T(8,128)(2,1)} %param.9) | copy-start | bytes 663556
  7.2 179.9 %all-reduce.3.cloned.1.call-start = ((), (), s32[]{:S(2)}) async-start(), calls=%async_computation | async-start | bytes 4718592 | tf_op jit(solution)/shard_map/psum | solution.py:310
  16.2 1.0 copy-start
  16.3 1.1 copy-start.1
  41.0 3.6 %copy-start.2 = (f32[576,192]{0,1:T(8,128)S(1)}, f32[576,192]{0,1:T(8,128)}, u32[]{:S(2)}) copy-start(f32[576,192]{0,1:T(8,128)} %copy.19) | copy-start | bytes 1327108
Sparse Core Ops, SparseCore 0:
  48.9 138.1 all-reduce.2
where the time goes:
time: 204 us; the launch traced here: 202 us
  waiting for transfers between devices  138 us (68%)
  local copies, waits for them, and re-layouts  25.1 us (12%)
  Pallas kernels  21.8 us (11%)
  between operations  14.9 us (7%)
  other arithmetic  2.23 us (1%)
    psum x1, waiting for transfers between devices, on_device(): s1, s2 = lax.psum((g1, g2), ('bricks', 'groups'))  138 us
    pallas_call x1, Pallas kernels, on_device(): pl.pallas_call(level_kernel, out_shape=(jax.ShapeDtypeStruct((slots, chan...  21.8 us
    rev x2, local copies, waits for them, and re-layouts, weight_out(): g = jnp.flip(g.reshape(3, 3, channels, 3, channels), (0, 1)) * factor  7.25 us
    unnamed x14, local copies, waits for them, and re-layouts  6.74 us
  transfers between devices with their start and end apart: 1, of which 1 were waited for; matrix products, arithmetic and copies ran while one was open for 0% of the time, Pallas kernels for 0%

commit v1 on v0

--- a/solution.py
+++ b/solution.py
@@ -29,10 +29,12 @@
 
 
 def level_kernel(
+    factor,
     count_ref, adj_ref, f_ref, c_ref, w1_ref, w2_ref, w3_ref,
-    out_ref, g1_ref, g2_ref,
+    out_ref, g1_out, g2_out,
     base, fx, t_ref, x9, zc, zd, f3, h3, y_ref, gate, hidden, halo0, halo1, halo2, halo3,
-    send_sem, recv_sem,
+    g1_ref, g2_ref, part, mid, total, from_groups, from_bricks,
+    send_sem, recv_sem, sum_send, sum_recv,
 ):
     slots, channels, cells = f_ref.shape
     count = cells // LANES
@@ -43,13 +45,40 @@
     halos = (halo0, halo1, halo2, halo3)
     barrier = pltpu.get_barrier_semaphore()
 
-    @pl.when(has_low)
-    def _():
-        pl.semaphore_signal(barrier, inc=1, device_id={"bricks": b - 1}, device_id_type=MESH)
-
-    @pl.when(has_up)
-    def _():
-        pl.semaphore_signal(barrier, inc=1, device_id={"bricks": b + 1}, device_id_type=MESH)
+    g = lax.axis_index("groups")
+    brick_count, group_count = lax.axis_size("bricks"), lax.axis_size("groups")
+
+    def greet(axis, me, size):
+        def one(k, carry):
+            pl.semaphore_signal(
+                barrier, inc=1, device_id={axis: lax.rem(me + k, size)}, device_id_type=MESH
+            )
+            return carry
+
+        lax.fori_loop(1, size, one, 0)
+
+    greet("bricks", b, brick_count)
+    greet("groups", g, group_count)
+
+    def exchange(phase, axis, me, size, src, dst):
+        def copy(k):
+            peer = lax.rem(me + k, size)
+            return pltpu.make_async_remote_copy(
+                src_ref=src(peer), dst_ref=dst(k),
+                send_sem=sum_send.at[phase, k], recv_sem=sum_recv.at[phase, k],
+                device_id={axis: peer}, device_id_type=MESH,
+            )
+
+        def start(k, carry):
+            copy(k).start()
+            return carry
+
+        def wait(k, carry):
+            copy(k).wait()
+            return carry
+
+        lax.fori_loop(1, size, start, 0)
+        return lambda: lax.fori_loop(1, size, wait, 0)
 
     def lanes(r):
         return lax.broadcasted_iota(jnp.int32, (r, LANES), 1)
@@ -107,16 +136,17 @@
 
         lax.fori_loop(0, slots, step, 0)
 
-    def stage(src, dst, s, k, parts, nrows):
+    def stage(src, dst, s, k, parts, nrows, sign=1):
         width = 8 if k == 1 else 1
         lane = lanes(nrows)
         coord = (lane // width) % 8
         low, up = local(s, k, -1), local(s, k, 1)
+        first, final = (0, 2 * nrows) if sign > 0 else (2 * nrows, 0)
         for j in range(parts):
             own = src[s, :, chunk(j)]
-            dst[0:nrows, chunk(j)] = shifted(own, src[low, :, chunk(j)], width, -1, coord)
+            dst[first:first + nrows, chunk(j)] = shifted(own, src[low, :, chunk(j)], width, -1, coord)
             dst[nrows:2 * nrows, chunk(j)] = own
-            dst[2 * nrows:3 * nrows, chunk(j)] = shifted(
+            dst[final:final + nrows, chunk(j)] = shifted(
                 own, src[up, :, chunk(j)], width, 1, coord
             )
 
@@ -127,7 +157,7 @@
         return jnp.where(lanes(channels) < 64, first, final).astype(BF)
 
     def combine(s, k, j):
-        zero, minus, plus = channels, 0, 2 * channels
+        zero, minus, plus = channels, 2 * channels, 0
         y_zero = y_ref[k, s, zero:zero + channels, chunk(j)]
         plus_here = y_ref[k, s, plus:plus + channels, chunk(j)]
         minus_here = y_ref[k, s, minus:minus + channels, chunk(j)]
@@ -167,18 +197,18 @@
 
     each_slot(mask_fields)
 
-    pl.semaphore_wait(barrier, has_low.astype(jnp.int32) + has_up.astype(jnp.int32))
+    pl.semaphore_wait(barrier, brick_count + group_count - 2)
     send(0)
 
     def back_conv(k, w_ref, z_ref):
-        each_slot(lambda s: stage(base, t_ref.at[s], s, 2, count, channels))
+        each_slot(lambda s: stage(base, t_ref.at[s], s, 2, count, channels, -1))
 
         def second(s):
-            stage(t_ref, z_ref.at[s], s, 1, count, rows)
+            stage(t_ref, z_ref.at[s], s, 1, count, rows, -1)
             y = jnp.dot(w_ref[...], z_ref[s], preferred_element_type=F32)
             y_ref[k, s] = y
             halos[1 + 2 * k][slots + s] = edges(
-                y[2 * channels:, chunk(0)], y[:channels, chunk(count - 1)]
+                y[:channels, chunk(0)], y[2 * channels:, chunk(count - 1)]
             )
 
         each_slot(second)
@@ -248,10 +278,31 @@
 
     def weight_grads(s):
         nt = (((1,), (1,)), ((), ()))
-        g2_ref[...] += lax.dot_general(zc[s], h3[s], nt, preferred_element_type=F32)
-        g1_ref[...] += lax.dot_general(zd[s], f3[s], nt, preferred_element_type=F32)
+        g2_ref[:, 0:rows] += lax.dot_general(zc[s], h3[s], nt, preferred_element_type=F32)
+        g1_ref[:, 0:rows] += lax.dot_general(zd[s], f3[s], nt, preferred_element_type=F32)
 
     each_slot(weight_grads)
+
+    units, unit_rows = part.shape[:2]
+    cols = g1_ref.shape[0]
+    span = cols // unit_rows
+    wide = lax.broadcasted_iota(jnp.int32, (cols, LANES), 1)
+
+    def put(at, value):
+        part[at * span:(at + 1) * span] = value.astype(BF).reshape(span, unit_rows, LANES)
+
+    put(0, g2_ref[:, 0:LANES])
+    put(1, g1_ref[:, 0:LANES])
+    put(2, jnp.where(
+        wide < 64, g2_ref[:, LANES:2 * LANES], pltpu.roll(g1_ref[:, LANES:2 * LANES], 64, 1)
+    ))
+    part[3 * span:] = jnp.zeros((units - 3 * span, unit_rows, LANES), BF)
+    own_units = pl.ds(g * brick_count, brick_count)
+    own_unit = g * brick_count + b
+    done = exchange(
+        0, "groups", g, group_count,
+        lambda peer: part.at[pl.ds(peer * brick_count, brick_count)], lambda k: from_groups.at[k],
+    )
     arrive(3)
 
     def finish(s):
@@ -259,6 +310,35 @@
             out_ref[s, :, chunk(j)] = combine(s, 1, j).astype(BF)
 
     each_slot(finish)
+    done()
+    acc = part[own_units].astype(F32)
+    for k in range(1, group_count):
+        acc = acc + from_groups[k].astype(F32)
+    mid[...] = acc.astype(BF)
+    exchange(
+        1, "bricks", b, brick_count, lambda peer: mid.at[peer], lambda k: from_bricks.at[k]
+    )()
+    acc = mid[b].astype(F32)
+    for k in range(1, brick_count):
+        acc = acc + from_bricks[k].astype(F32)
+    total[own_unit] = (acc * factor).astype(BF)
+    exchange(
+        2, "bricks", b, brick_count,
+        lambda peer: total.at[own_unit], lambda k: total.at[own_unit],
+    )()
+    exchange(
+        3, "groups", g, group_count,
+        lambda peer: total.at[own_units], lambda k: total.at[own_units],
+    )()
+
+    def get(at):
+        return total[at * span:(at + 1) * span].reshape(cols, LANES).astype(F32)
+
+    g2_out[:, 0:LANES] = get(0)
+    g1_out[:, 0:LANES] = get(1)
+    mixed = get(2)
+    g2_out[:, LANES:rows] = mixed[:, 0:rows - LANES]
+    g1_out[:, LANES:rows] = pltpu.roll(mixed, 64, 1)[:, 0:rows - LANES]
 
 
 def on_device(fields, cotangent, first_weight, second_weight, counts, adjacency):
@@ -269,12 +349,20 @@
     forward_w = jnp.transpose(w1, (2, 0, 4, 3, 1)).reshape(rows, cols)
 
     def backward_w(w):
-        return jnp.transpose(jnp.flip(w, (2, 3, 4)), (2, 1, 3, 4, 0)).reshape(rows, cols)
-
+        return jnp.transpose(w, (2, 1, 3, 4, 0)).reshape(rows, cols)
+
+    brick_count, group_count = lax.axis_size("bricks"), lax.axis_size("groups")
+    factor = float((group_count * slots * brick_count * cells) ** -0.5)
+    devices = brick_count * group_count
+    unit_rows = 16
+    while devices * unit_rows * LANES < 2 * rows * cols or cols % unit_rows:
+        unit_rows += 16
+    unit = (unit_rows, LANES)
+    peers = max(brick_count, group_count)
     vmem = pl.BlockSpec(memory_space=pltpu.VMEM)
     smem = pl.BlockSpec(memory_space=pltpu.SMEM)
     grad_fields, g1, g2 = pl.pallas_call(
-        level_kernel,
+        functools.partial(level_kernel, factor),
         out_shape=(
             jax.ShapeDtypeStruct((slots, channels, cells), BF),
             jax.ShapeDtypeStruct((cols, rows), F32),
@@ -297,8 +385,17 @@
         ]
         + [pltpu.VMEM((3 * slots + 1, channels, LANES), BF)] * 4
         + [
+            pltpu.VMEM((cols, 2 * LANES), F32),
+            pltpu.VMEM((cols, 2 * LANES), F32),
+            pltpu.VMEM((devices,) + unit, BF),
+            pltpu.VMEM((brick_count,) + unit, BF),
+            pltpu.VMEM((devices,) + unit, BF),
+            pltpu.VMEM((group_count, brick_count) + unit, BF),
+            pltpu.VMEM((brick_count,) + unit, BF),
             pltpu.SemaphoreType.DMA((4, 2)),
             pltpu.SemaphoreType.DMA((4, 2)),
+            pltpu.SemaphoreType.DMA((4, peers)),
+            pltpu.SemaphoreType.DMA((4, peers)),
         ],
         compiler_params=pltpu.CompilerParams(
             collective_id=0, has_side_effects=True, vmem_limit_bytes=50 * 1024 * 1024
@@ -307,15 +404,11 @@
         counts, adjacency[0], fields[0], cotangent[0],
         forward_w, backward_w(w2), backward_w(w1),
     )
-    s1, s2 = lax.psum((g1, g2), ("bricks", "groups"))
-    total = lax.axis_size("groups") * slots * lax.axis_size("bricks") * cells
-    factor = 1.0 / jnp.sqrt(jnp.float32(total))
-
     def weight_out(g):
-        g = jnp.flip(g.reshape(3, 3, channels, 3, channels), (0, 1)) * factor
+        g = g.reshape(3, 3, channels, 3, channels)
         return jnp.transpose(g, (2, 4, 3, 0, 1)).reshape(channels, channels * 27)
 
-    return (grad_fields[None], weight_out(s1), weight_out(s2))
+    return (grad_fields[None], weight_out(g1), weight_out(g2))
 
 
 def solution(mesh):

time: 204 us -> 63.8 us (0.31)
  waiting for transfers between devices: 138 us -> 0 us
  Pallas kernels: 21.8 us -> 49.9 us
  between operations: 14.9 us -> 1.49 us
  local copies, waits for them, and re-layouts: 25.1 us -> 12.1 us
  other arithmetic: 2.23 us -> 0 us
    psum x1 -> x0, waiting for transfers between devices: 138 us -> none  [on_device(): s1, s2 = lax.psum((g1, g2), ('bricks', 'groups'))]
    pallas_call x1, Pallas kernels: 21.8 us -> 49.9 us  [on_device(): pl.pallas_call(functools.partial(level_kernel, factor), out_shape=(jax.Sh...]
    rev x4 -> x0, local copies, waits for them, and re-layouts: 10.7 us -> none  [the longest x2 7.25 us: weight_out(): g = jnp.flip(g.reshape(3, 3, channels, 3, channels), (0, 1)) * factor]
    transpose x1 -> x0, other arithmetic: 2.23 us -> none  [weight_out(): return jnp.transpose(g, (2, 4, 3, 0, 1)).reshape(channels, channels * 27)]
  transfers between devices with their start and end apart: 1 -> 0, of which waited for: 1 -> 0; matrix products, arithmetic and copies ran while one was open for 0% -> 0% of each run, Pallas kernels for 0% -> 0%
where the time goes in v1:
time: 63.8 us; the launch traced here: 63.5 us
  Pallas kernels  49.9 us (78%)
  local copies, waits for them, and re-layouts  12.1 us (19%)
  between operations  1.49 us (2%)
    pallas_call x1, Pallas kernels, on_device(): pl.pallas_call(functools.partial(level_kernel, factor), out_shape=(jax.Sh...  49.9 us
    unnamed x14, local copies, waits for them, and re-layouts  5.51 us

profile of v1, /device:TPU:1, one launch (start us, length us, event | category | flops | bytes accessed | tf_op | source)
XLA Modules:
  0.0 63.5 jit_solution(17194891876527710821)
XLA Ops:
  0.6 0.0 copy-start.3
  1.3 0.7 %copy.27 = s32[1,6,6]{2,1,0:T(8,128)S(1)} copy(s32[1,6,6]{2,0,1:T(1,128)} %param.11) | data formatting | bytes 288
  2.0 1.2 %copy.14 = bf16[64,1728]{0,1:T(8,128)(2,1)S(1)} copy(bf16[64,1728]{1,0:T(8,128)(2,1)} %param.8) | data formatting | bytes 442368 | tf_op args[2]
  3.2 0.3 reshape.33
  3.5 0.0 copy-done.3
  3.5 0.3 copy.16
  3.8 0.3 reshape.35
  4.0 0.2 copy.17
  4.3 0.4 reshape.36.w2_ref
  4.7 1.0 %copy.15 = bf16[3,64,3,3,64]{4,3,2,1,0:T(4,128)(2,1)S(1)} copy(bf16[3,64,3,3,64]{1,2,3,0,4:T(4,128)(2,1)S(1)} %bitcast.27) | data formatting | bytes 442368 | tf_op jit(solution)/shard_map/transpose | solution.py:349
  5.7 0.4 reshape.34.w1_ref
  6.1 0.0 copy-start
  6.1 0.0 copy-start.1
  6.1 0.2 copy.18
  6.3 0.4 reshape.37.w3_ref
  6.7 0.4 copy-done
  7.1 0.1 copy-done.1
  7.2 49.9 %shard_map.85 = (bf16[6,64,512]{2,1,0:T(8,128)(2,1)S(1)}, f32[576,192]{1,0:T(8,128)S(1)}, f32[576,192]{1,0:T(8,128)S(1)}) custom-call(s32[1,1]{1,0:T(1,128)S(6)} %copy.29.count_ref, s32[6,6]{1,0:T(8,128)S(1)} %bitcast.26, bf16[6,64,512]{2,1,0:T(8,128)(2,1)S(1)} %bitcast.24, bf16[6,64,512]{2,1,0:T(8,128)(2,1)S(1)} %bitcast.25, ...), custom_call_target="tpu_custom_call" | custom-call | tf_op jit(solution)/shard_map/pallas_call | solution.py:364
  57.2 1.0 %copy.19 = f32[576,192]{0,1:T(8,128)} copy(f32[576,192]{1,0:T(8,128)S(1)} %get-tuple-element.7) | data formatting | bytes 884736 | tf_op jit(solution)/shard_map/pallas_call | solution.py:364
  58.2 0.2 copy.21
  58.4 0.5 reshape.40
  58.9 0.2 copy.22
  59.1 0.4 reshape.41
  59.5 0.0 copy-start.2
  59.5 1.1 %copy.24 = f32[64,1728]{1,0:T(8,128)} copy(f32[64,1728]{0,1:T(8,128)S(1)} %reshape.41) | data formatting | bytes 884736
  60.6 0.0 copy-done.2
  60.6 0.5 reshape.38
  61.1 0.2 copy.20
  61.3 0.4 reshape.39
  61.7 1.1 %copy.23 = f32[64,1728]{1,0:T(8,128)} copy(f32[64,1728]{0,1:T(8,128)S(1)} %reshape.39) | data formatting | bytes 884736
  62.8 0.7 %copy.30 = bf16[1,6,64,512]{3,2,1,0:T(8,128)(2,1)} copy(bf16[1,6,64,512]{3,2,1,0:T(8,128)(2,1)S(1)} %bitcast.23) | data formatting | bytes 786432
Async XLA Ops:
  0.6 2.9 %copy-start.3 = (bf16[64,1728]{1,0:T(8,128)(2,1)S(1)}, bf16[64,1728]{1,0:T(8,128)(2,1)}, u32[]{:S(2)}) copy-start(bf16[64,1728]{1,0:T(8,128)(2,1)} %param.9) | copy-start | bytes 663556
  6.1 1.0 %copy-start = (bf16[1,6,64,512]{3,2,1,0:T(8,128)(2,1)S(1)}, bf16[1,6,64,512]{3,2,1,0:T(8,128)(2,1)}, u32[]{:S(2)}) copy-start(bf16[1,6,64,512]{3,2,1,0:T(8,128)(2,1)} %param.6) | copy-start | bytes 1179652
  6.1 1.1 %copy-start.1 = (bf16[1,6,64,512]{3,2,1,0:T(8,128)(2,1)S(1)}, bf16[1,6,64,512]{3,2,1,0:T(8,128)(2,1)}, u32[]{:S(2)}) copy-start(bf16[1,6,64,512]{3,2,1,0:T(8,128)(2,1)} %param.7) | copy-start | bytes 1179652
  59.5 1.1 %copy-start.2 = (f32[576,192]{0,1:T(8,128)S(1)}, f32[576,192]{0,1:T(8,128)}, u32[]{:S(2)}) copy-start(f32[576,192]{0,1:T(8,128)} %copy.19) | copy-start | bytes 1327108

commit v2 on v1

--- a/solution.py
+++ b/solution.py
@@ -33,9 +33,10 @@
     count_ref, adj_ref, f_ref, c_ref, w1_ref, w2_ref, w3_ref,
     out_ref, g1_out, g2_out,
     base, fx, t_ref, x9, zc, zd, f3, h3, y_ref, gate, hidden, halo0, halo1, halo2, halo3,
-    g1_ref, g2_ref, part, mid, total, from_groups, from_bricks,
-    send_sem, recv_sem, sum_send, sum_recv,
+    g1_ref, g2_ref, *rest,
 ):
+    buffers = rest[:5], rest[5:10]
+    send_sem, recv_sem, sum_send, sum_recv = rest[10:]
     slots, channels, cells = f_ref.shape
     count = cells // LANES
     b = lax.axis_index("bricks")
@@ -258,7 +259,6 @@
             base[s, :, chunk(j)] = (combine(s, 0, j) * gate[s, :, chunk(j)]).astype(BF)
 
     each_slot(d_pre)
-    back_conv(1, w3_ref, zd)
     arrive(2)
 
     def widen_hidden(s):
@@ -273,36 +273,86 @@
                 h3[s, 2 * channels:3 * channels, chunk(j - 1)] = part
 
     each_slot(widen_hidden)
-    g1_ref[...] = jnp.zeros_like(g1_ref)
-    g2_ref[...] = jnp.zeros_like(g2_ref)
-
-    def weight_grads(s):
-        nt = (((1,), (1,)), ((), ()))
-        g2_ref[:, 0:rows] += lax.dot_general(zc[s], h3[s], nt, preferred_element_type=F32)
-        g1_ref[:, 0:rows] += lax.dot_general(zd[s], f3[s], nt, preferred_element_type=F32)
-
-    each_slot(weight_grads)
-
-    units, unit_rows = part.shape[:2]
-    cols = g1_ref.shape[0]
-    span = cols // unit_rows
-    wide = lax.broadcasted_iota(jnp.int32, (cols, LANES), 1)
-
-    def put(at, value):
-        part[at * span:(at + 1) * span] = value.astype(BF).reshape(span, unit_rows, LANES)
-
-    put(0, g2_ref[:, 0:LANES])
-    put(1, g1_ref[:, 0:LANES])
-    put(2, jnp.where(
-        wide < 64, g2_ref[:, LANES:2 * LANES], pltpu.roll(g1_ref[:, LANES:2 * LANES], 64, 1)
-    ))
-    part[3 * span:] = jnp.zeros((units - 3 * span, unit_rows, LANES), BF)
     own_units = pl.ds(g * brick_count, brick_count)
     own_unit = g * brick_count + b
-    done = exchange(
-        0, "groups", g, group_count,
-        lambda peer: part.at[pl.ds(peer * brick_count, brick_count)], lambda k: from_groups.at[k],
-    )
+    cols = g1_ref.shape[0]
+    half = cols // 2
+    low_lanes = lax.broadcasted_iota(jnp.int32, (half, LANES), 1) < 64
+
+    def weight_grad(acc_ref, z_ref, source):
+        acc_ref[...] = jnp.zeros_like(acc_ref)
+
+        def add(s):
+            acc_ref[:, 0:rows] += lax.dot_general(
+                z_ref[s], source[s], (((1,), (1,)), ((), ())), preferred_element_type=F32
+            )
+
+        each_slot(add)
+
+    def scatter_groups(i, acc_ref):
+        part, from_groups = buffers[i][0], buffers[i][3]
+        units, unit_rows = part.shape[:2]
+        first, used = cols // unit_rows, 3 * half // unit_rows
+        part[0:first] = acc_ref[:, 0:LANES].astype(BF).reshape(first, unit_rows, LANES)
+        packed = jnp.where(
+            low_lanes, acc_ref[0:half, LANES:2 * LANES],
+            pltpu.roll(acc_ref[half:cols, LANES:2 * LANES], 64, 1),
+        )
+        part[first:used] = packed.astype(BF).reshape(used - first, unit_rows, LANES)
+        part[used:] = jnp.zeros((units - used, unit_rows, LANES), BF)
+        return exchange(
+            4 * i, "groups", g, group_count,
+            lambda peer: part.at[pl.ds(peer * brick_count, brick_count)],
+            lambda k: from_groups.at[k],
+        )
+
+    def scatter_bricks(i):
+        part, mid, _, from_groups, from_bricks = buffers[i]
+        acc = part[own_units].astype(F32)
+        for k in range(1, group_count):
+            acc = acc + from_groups[k].astype(F32)
+        mid[...] = acc.astype(BF)
+        return exchange(
+            4 * i + 1, "bricks", b, brick_count,
+            lambda peer: mid.at[peer], lambda k: from_bricks.at[k],
+        )
+
+    def gather_bricks(i):
+        _, mid, total, _, from_bricks = buffers[i]
+        acc = mid[b].astype(F32)
+        for k in range(1, brick_count):
+            acc = acc + from_bricks[k].astype(F32)
+        total[own_unit] = (acc * factor).astype(BF)
+        return exchange(
+            4 * i + 2, "bricks", b, brick_count,
+            lambda peer: total.at[own_unit], lambda k: total.at[own_unit],
+        )
+
+    def gather_groups(i):
+        total = buffers[i][2]
+        return exchange(
+            4 * i + 3, "groups", g, group_count,
+            lambda peer: total.at[own_units], lambda k: total.at[own_units],
+        )
+
+    def unpack(i, out):
+        total = buffers[i][2]
+        unit_rows = total.shape[1]
+        first, used = cols // unit_rows, 3 * half // unit_rows
+        out[:, 0:LANES] = total[0:first].reshape(cols, LANES).astype(F32)
+        packed = total[first:used].reshape(half, LANES).astype(F32)
+        out[0:half, LANES:rows] = packed[:, 0:rows - LANES]
+        out[half:cols, LANES:rows] = pltpu.roll(packed, 64, 1)[:, 0:rows - LANES]
+
+    weight_grad(g2_ref, zc, h3)
+    second_done = scatter_groups(0, g2_ref)
+    back_conv(1, w3_ref, zd)
+    second_done()
+    second_done = scatter_bricks(0)
+    weight_grad(g1_ref, zd, f3)
+    first_done = scatter_groups(1, g1_ref)
+    second_done()
+    second_done = gather_bricks(0)
     arrive(3)
 
     def finish(s):
@@ -310,35 +360,17 @@
             out_ref[s, :, chunk(j)] = combine(s, 1, j).astype(BF)
 
     each_slot(finish)
-    done()
-    acc = part[own_units].astype(F32)
-    for k in range(1, group_count):
-        acc = acc + from_groups[k].astype(F32)
-    mid[...] = acc.astype(BF)
-    exchange(
-        1, "bricks", b, brick_count, lambda peer: mid.at[peer], lambda k: from_bricks.at[k]
-    )()
-    acc = mid[b].astype(F32)
-    for k in range(1, brick_count):
-        acc = acc + from_bricks[k].astype(F32)
-    total[own_unit] = (acc * factor).astype(BF)
-    exchange(
-        2, "bricks", b, brick_count,
-        lambda peer: total.at[own_unit], lambda k: total.at[own_unit],
-    )()
-    exchange(
-        3, "groups", g, group_count,
-        lambda peer: total.at[own_units], lambda k: total.at[own_units],
-    )()
-
-    def get(at):
-        return total[at * span:(at + 1) * span].reshape(cols, LANES).astype(F32)
-
-    g2_out[:, 0:LANES] = get(0)
-    g1_out[:, 0:LANES] = get(1)
-    mixed = get(2)
-    g2_out[:, LANES:rows] = mixed[:, 0:rows - LANES]
-    g1_out[:, LANES:rows] = pltpu.roll(mixed, 64, 1)[:, 0:rows - LANES]
+    first_done()
+    first_done = scatter_bricks(1)
+    second_done()
+    second_done = gather_groups(0)
+    first_done()
+    first_done = gather_bricks(1)
+    second_done()
+    unpack(0, g2_out)
+    first_done()
+    gather_groups(1)()
+    unpack(1, g1_out)
 
 
 def on_device(fields, cotangent, first_weight, second_weight, counts, adjacency):
@@ -355,7 +387,7 @@
     factor = float((group_count * slots * brick_count * cells) ** -0.5)
     devices = brick_count * group_count
     unit_rows = 16
-    while devices * unit_rows * LANES < 2 * rows * cols or cols % unit_rows:
+    while devices * unit_rows * LANES < rows * cols or cols // 2 % unit_rows:
         unit_rows += 16
     unit = (unit_rows, LANES)
     peers = max(brick_count, group_count)
@@ -392,10 +424,15 @@
             pltpu.VMEM((devices,) + unit, BF),
             pltpu.VMEM((group_count, brick_count) + unit, BF),
             pltpu.VMEM((brick_count,) + unit, BF),
+            pltpu.VMEM((devices,) + unit, BF),
+            pltpu.VMEM((brick_count,) + unit, BF),
+            pltpu.VMEM((devices,) + unit, BF),
+            pltpu.VMEM((group_count, brick_count) + unit, BF),
+            pltpu.VMEM((brick_count,) + unit, BF),
             pltpu.SemaphoreType.DMA((4, 2)),
             pltpu.SemaphoreType.DMA((4, 2)),
-            pltpu.SemaphoreType.DMA((4, peers)),
-            pltpu.SemaphoreType.DMA((4, peers)),
+            pltpu.SemaphoreType.DMA((8, peers)),
+            pltpu.SemaphoreType.DMA((8, peers)),
         ],
         compiler_params=pltpu.CompilerParams(
             collective_id=0, has_side_effects=True, vmem_limit_bytes=50 * 1024 * 1024

time: 63.8 us -> 64.5 us (1.011)
  Pallas kernels: 49.9 us -> 50.6 us
    pallas_call x1, Pallas kernels: 49.9 us -> 50.6 us  [on_device(): pl.pallas_call(functools.partial(level_kernel, factor), out_shape=(jax.Sh...]
where the time goes in v2:
time: 64.5 us; the launch traced here: 64.2 us
  Pallas kernels  50.6 us (78%)
  local copies, waits for them, and re-layouts  12.1 us (19%)
  between operations  1.49 us (2%)
    pallas_call x1, Pallas kernels, on_device(): pl.pallas_call(functools.partial(level_kernel, factor), out_shape=(jax.Sh...  50.6 us
    unnamed x14, local copies, waits for them, and re-layouts  5.51 us

profile of v2, /device:TPU:1, one launch (start us, length us, event | category | flops | bytes accessed | tf_op | source)
XLA Modules:
  0.0 64.2 jit_solution(6680872890620918322)
XLA Ops:
  0.6 0.0 copy-start.3
  1.3 0.7 %copy.27 = s32[1,6,6]{2,1,0:T(8,128)S(1)} copy(s32[1,6,6]{2,0,1:T(1,128)} %param.11) | data formatting | bytes 288
  2.0 1.2 %copy.14 = bf16[64,1728]{0,1:T(8,128)(2,1)S(1)} copy(bf16[64,1728]{1,0:T(8,128)(2,1)} %param.8) | data formatting | bytes 442368 | tf_op args[2]
  3.2 0.3 reshape.33
  3.5 0.0 copy-done.3
  3.5 0.3 copy.16
  3.8 0.3 reshape.35
  4.0 0.2 copy.17
  4.3 0.4 reshape.36.w2_ref
  4.7 1.0 %copy.15 = bf16[3,64,3,3,64]{4,3,2,1,0:T(4,128)(2,1)S(1)} copy(bf16[3,64,3,3,64]{1,2,3,0,4:T(4,128)(2,1)S(1)} %bitcast.27) | data formatting | bytes 442368 | tf_op jit(solution)/shard_map/transpose | solution.py:381
  5.7 0.4 reshape.34.w1_ref
  6.1 0.0 copy-start
  6.1 0.0 copy-start.1
  6.1 0.2 copy.18
  6.3 0.4 reshape.37.w3_ref
  6.7 0.4 copy-done
  7.1 0.1 copy-done.1
  7.2 50.6 %shard_map.85 = (bf16[6,64,512]{2,1,0:T(8,128)(2,1)S(1)}, f32[576,192]{1,0:T(8,128)S(1)}, f32[576,192]{1,0:T(8,128)S(1)}) custom-call(s32[1,1]{1,0:T(1,128)S(6)} %copy.29.count_ref, s32[6,6]{1,0:T(8,128)S(1)} %bitcast.26, bf16[6,64,512]{2,1,0:T(8,128)(2,1)S(1)} %bitcast.24, bf16[6,64,512]{2,1,0:T(8,128)(2,1)S(1)} %bitcast.25, ...), custom_call_target="tpu_custom_call" | custom-call | tf_op jit(solution)/shard_map/pallas_call | solution.py:396
  57.9 1.0 %copy.19 = f32[576,192]{0,1:T(8,128)} copy(f32[576,192]{1,0:T(8,128)S(1)} %get-tuple-element.7) | data formatting | bytes 884736 | tf_op jit(solution)/shard_map/pallas_call | solution.py:396
  58.9 0.2 copy.21
  59.1 0.5 reshape.40
  59.6 0.2 copy.22
  59.8 0.4 reshape.41
  60.2 0.0 copy-start.2
  60.2 1.1 %copy.24 = f32[64,1728]{1,0:T(8,128)} copy(f32[64,1728]{0,1:T(8,128)S(1)} %reshape.41) | data formatting | bytes 884736
  61.3 0.0 copy-done.2
  61.3 0.5 reshape.38
  61.8 0.2 copy.20
  62.0 0.4 reshape.39
  62.4 1.1 %copy.23 = f32[64,1728]{1,0:T(8,128)} copy(f32[64,1728]{0,1:T(8,128)S(1)} %reshape.39) | data formatting | bytes 884736
  63.5 0.7 %copy.30 = bf16[1,6,64,512]{3,2,1,0:T(8,128)(2,1)} copy(bf16[1,6,64,512]{3,2,1,0:T(8,128)(2,1)S(1)} %bitcast.23) | data formatting | bytes 786432
Async XLA Ops:
  0.6 2.9 %copy-start.3 = (bf16[64,1728]{1,0:T(8,128)(2,1)S(1)}, bf16[64,1728]{1,0:T(8,128)(2,1)}, u32[]{:S(2)}) copy-start(bf16[64,1728]{1,0:T(8,128)(2,1)} %param.9) | copy-start | bytes 663556
  6.1 1.0 %copy-start = (bf16[1,6,64,512]{3,2,1,0:T(8,128)(2,1)S(1)}, bf16[1,6,64,512]{3,2,1,0:T(8,128)(2,1)}, u32[]{:S(2)}) copy-start(bf16[1,6,64,512]{3,2,1,0:T(8,128)(2,1)} %param.6) | copy-start | bytes 1179652
  6.1 1.1 %copy-start.1 = (bf16[1,6,64,512]{3,2,1,0:T(8,128)(2,1)S(1)}, bf16[1,6,64,512]{3,2,1,0:T(8,128)(2,1)}, u32[]{:S(2)}) copy-start(bf16[1,6,64,512]{3,2,1,0:T(8,128)(2,1)} %param.7) | copy-start | bytes 1179652
  60.2 1.1 %copy-start.2 = (f32[576,192]{0,1:T(8,128)S(1)}, f32[576,192]{0,1:T(8,128)}, u32[]{:S(2)}) copy-start(f32[576,192]{0,1:T(8,128)} %copy.19) | copy-start | bytes 1327108
